TPU v7x, 32 devices: a whole 2x2x4 slice. The times are simulated.
32 devices in a mesh: dp: 16 (over z, y, x), cuts: 2 (over core).
Axes of the slice: x: 2, y: 2, z: 4, core: 2. Of those that a mesh axis runs over, the one named last changes fastest.
Arguments:
- activations: bfloat16 [12288, 8192], P('dp', 'cuts'), may hold values from -6 to 6
- out_grads: bfloat16 [12288, 512], P('dp'), may hold values from -0.16210938 to 0.16210938
- weight: bfloat16 [512, 8192], P('dp', 'cuts'), may hold values from -0.0625 to 0.0625
- left_basis: bfloat16 [16, 512, 512], P('cuts'), may hold values from -0.25 to 0.25
- right_basis: bfloat16 [16, 512, 512], P('cuts'), may hold values from -0.25 to 0.25
- first_moment: float32 [512, 16, 512], P('dp', 'cuts'), may hold values from -3 to 3
- second_moment: float32 [512, 16, 512], P('dp', 'cuts'), may hold values from 0.05 to 2
Outputs:
- layer_output: bfloat16 [12288, 512], P('dp', 'cuts')
- new_weight: bfloat16 [512, 8192], P('dp', 'cuts')
- new_first: float32 [512, 16, 512], P('dp', 'cuts')
- new_second: float32 [512, 16, 512], P('dp', 'cuts')
All inputs are finite; a program needn't handle non-finite values.
Results may differ from a plain program's by a relative error of at most 0.0048.
Values may be sent and summed in bfloat16 or wider, within the bound.
A program may use at most 128 MiB of HBM per device.

v0:
```python
import jax
import jax.numpy as jnp
from jax import lax
from jax.sharding import PartitionSpec as P

STEP = 10


LEARNING_RATE = 0.02
epsilon = 1e-08


def local(activations, out_grads, weight, left_basis, right_basis, first_moment, second_moment):
    highest = lax.Precision.HIGHEST
    left_full = left_basis.astype(jnp.float32)
    right_full = right_basis.astype(jnp.float32)
    num_blocks = left_full.shape[0]
    block_rows = left_full.shape[1]
    grad_slab = lax.psum_scatter(
        lax.dot_general(
            out_grads, activations, (((0,), (0,)), ((), ())), preferred_element_type=jnp.float32
        ),
        "dp",
        scatter_dimension=0,
        tiled=True,
    )
    grad_slab = grad_slab.reshape(grad_slab.shape[0], num_blocks, block_rows)
    left_turned = jnp.einsum("cbr,brk->cbk", grad_slab, left_full, precision=highest)
    regrouped = lax.all_to_all(left_turned, "dp", split_axis=2, concat_axis=0, tiled=True)
    rotated = jnp.einsum("cbk,bcd->kbd", regrouped, right_full, precision=highest)
    new_first = 0.9 * first_moment + 0.1 * rotated
    new_second = 0.95 * second_moment + 0.05 * rotated * rotated
    bias_first = 1.0 - 0.9**STEP
    bias_second = 1.0 - 0.95**STEP
    direction = new_first / bias_first / (jnp.sqrt(new_second / bias_second) + epsilon)
    back_turned = jnp.einsum("kbd,bcd->kbc", direction, right_full, precision=highest)
    returned = lax.all_to_all(back_turned, "dp", split_axis=2, concat_axis=0, tiled=True)
    update = jnp.einsum("kbc,brk->cbr", returned, left_full, precision=highest).reshape(
        weight.shape
    )
    new_weight = (weight.astype(jnp.float32) - LEARNING_RATE * update).astype(jnp.bfloat16)
    partial_out = lax.dot_general(
        activations,
        lax.all_gather(new_weight, "dp", axis=0, tiled=True),
        (((1,), (1,)), ((), ())),
        preferred_element_type=jnp.float32,
    )
    layer_output = lax.psum_scatter(partial_out, "cuts", scatter_dimension=1, tiled=True).astype(
        jnp.bfloat16
    )
    return (layer_output, new_weight, new_first, new_second)


def solution(mesh):
    placed = (
        P("dp", "cuts"),
        P("dp", None),
        P("dp", "cuts"),
        P("cuts", None, None),
        P("cuts", None, None),
        P("dp", "cuts", None),
        P("dp", "cuts", None),
    )
    return jax.shard_map(
        local,
        mesh=mesh,
        in_specs=placed,
        out_specs=(P("dp", "cuts"), P("dp", "cuts"), P("dp", "cuts", None), P("dp", "cuts", None)),
        check_vma=False,
    )
```

profile of v0, /device:TPU:0, one launch (start us, length us, event | category | flops | bytes accessed | tf_op | source)
XLA Modules:
  0.0 382.2 jit_solution(15899882490268071148)
XLA Ops:
  7.2 0.0 copy-start
  7.2 0.0 reduce-scatter.3.cloned.1.call-start
  7.2 1.1 copy-done
  8.3 8.4 %fusion.16 = f32[512,4096]{1,0:T(8,128)} fusion(bf16[768,512]{1,0:T(8,128)(2,1)S(1)} %copy-done, bf16[768,4096]{1,0:T(8,128)(2,1)} %param.7), kind=kOutput, calls=%fused_computation.27 | convolution fusion | flops 3221225472 | bytes 15466496 | tf_op jit(solution)/shard_map/dot_general | solution.py:20
  16.7 0.0 reduce-scatter.3.cloned.1.call-update
  16.8 0.0 all-gather.2.cloned.1.call-start
  16.8 180.6 %reduce-scatter.3.cloned.1.call-done = f32[32,4096]{1,0:T(8,128)} async-done(((f32[512,4096]{1,0:T(8,128)}), f32[32,4096]{1,0:T(8,128)}) %reduce-scatter.3.cloned.1.call-update) | async-done | bytes 524304 | tf_op jit(solution)/shard_map/reduce_scatter | solution.py:19
  197.4 4.4 %convolution_bitcast_fusion.3 = f32[32,8,512]{2,0,1:T(8,128)S(1)} fusion(bf16[8,512,512]{2,1,0:T(8,128)(2,1)} %param.10, f32[4,8,8,512]{3,2,1,0:T(8,128)} %bitcast.53), kind=kOutput, calls=%fused_computation.7 | convolution fusion | flops 805306368 | bytes 5242880 | tf_op jit(solution)/shard_map/cbr,brk->cbk/dot_general | solution.py:28
  201.9 0.8 copy.30
  202.7 0.9 reshape.15
  203.6 22.7 %all_to_all.36 = f32[16,1,8192]{2,1,0:T(1,128)S(1)} all-to-all(f32[16,1,8192]{2,1,0:T(1,128)S(1)} %reshape.15), channel_id=1, replica_groups=mesh['dp'=16,'cuts'=2] {'dp'}, dimensions={0} | all-to-all | bytes 1048576 | tf_op jit(solution)/shard_map/all_to_all | solution.py:29
  226.3 0.5 broadcast.6
  226.8 1.9 reduce
  228.7 0.7 reshape.16
  229.4 2.6 copy.54
  231.9 2.3 all_to_all.29
  234.2 0.0 copy-start.1
  234.2 5.0 %fusion.4 = (f32[32,8,512]{2,0,1:T(8,128)S(1)}, f32[32,8,512]{2,0,1:T(8,128)S(1)}) fusion(f32[32,8,512]{2,1,0:T(8,128)} %param.12, f32[32,8,512]{2,1,0:T(8,128)} %param.13, f32[512,8,32]{0,2,1:T(8,128)S(1)} %all_to_all.29, bf16[8,512,512]{2,1,0:T(8,128)(2,1)} %param.11), kind=kOutput, calls=%fused_computation.14 | convolution fusion | flops 806223872 | bytes 6815744 | tf_op jit(solution)/shard_map/cbk,bcd->kbd/dot_general | solution.py:30
  239.3 0.0 copy-start.2
  239.3 0.8 copy-done.2
  240.1 0.0 copy-done.1
  240.1 4.5 %convolution_bitcast_fusion.1 = f32[32,8,512]{2,0,1:T(8,128)} fusion(bf16[8,512,512]{2,1,0:T(8,128)(2,1)S(1)} %copy-done.1, f32[32,8,512]{2,0,1:T(8,128)S(1)} %get-tuple-element.17, f32[32,8,512]{2,0,1:T(8,128)S(1)} %get-tuple-element.16), kind=kOutput, calls=%fused_computation.5 | convolution fusion | flops 805830656 | bytes 5767168 | tf_op jit(solution)/shard_map/kbd,bcd->kbc/dot_general | solution.py:36
  244.5 1.8 copy.33
  246.4 1.7 reshape.17
  248.1 18.3 %all_to_all.37 = f32[16,1,8192]{2,1,0:T(1,128)S(1)} all-to-all(f32[16,1,8192]{2,1,0:T(1,128)} %reshape.17), channel_id=1, replica_groups=mesh['dp'=16,'cuts'=2] {'dp'}, dimensions={0} | all-to-all | bytes 1048576 | tf_op jit(solution)/shard_map/all_to_all | solution.py:37
  266.4 2.8 reduce.1
  269.2 1.7 reshape.18
  270.9 2.6 copy.53
  273.5 0.0 copy-start.4
  273.5 2.3 all_to_all.33
  275.8 5.9 %fusion = f32[8,4,8,512]{3,2,1,0:T(8,128)S(1)} fusion(f32[512,8,32]{0,2,1:T(8,128)S(1)} %all_to_all.33, bf16[8,512,512]{2,1,0:T(8,128)(2,1)} %param.10), kind=kOutput, calls=%fused_computation.4 | convolution fusion | flops 805437440 | bytes 5242880 | tf_op jit(solution)/shard_map/kbc,brk->cbr/dot_general | solution.py:38
  281.7 0.0 copy-done.4
  281.8 0.8 subtract_convert_fusion
  282.5 0.0 all-gather.2.cloned.1.call-update
  282.5 0.0 copy-start.3
  282.5 0.0 reduce-scatter.5.cloned.1.call-start
  282.6 74.4 %all-gather.2.cloned.1.call-done = bf16[512,4096]{1,0:T(8,128)(2,1)} async-done(((bf16[32,4096]{1,0:T(8,128)(2,1)}), bf16[512,4096]{1,0:T(8,128)(2,1)}) %all-gather.2.cloned.1.call-update) | async-done | bytes 4194320 | tf_op jit(solution)/shard_map/all_gather | solution.py:44
  357.0 8.7 %convolution_bitcast_fusion = f32[768,512]{0,1:T(8,128)} fusion(bf16[512,4096]{1,0:T(8,128)(2,1)} %all-gather.2.cloned.1.call-done, bf16[768,4096]{1,0:T(8,128)(2,1)} %param.7), kind=kOutput, calls=%fused_computation.2 | convolution fusion | flops 3221225472 | bytes 12058624 | tf_op jit(solution)/shard_map/dot_general | solution.py:42
  365.7 0.0 reduce-scatter.5.cloned.1.call-update
  365.7 0.0 copy-done.3
  365.7 1.1 copy.37
  366.8 1.1 copy.38
  367.9 5.6 %reduce-scatter.5.cloned.1.call-done = f32[768,256]{0,1:T(8,128)} async-done(((f32[768,512]{0,1:T(8,128)}), f32[768,256]{0,1:T(8,128)}) %reduce-scatter.5.cloned.1.call-update) | async-done | bytes 786448 | tf_op jit(solution)/shard_map/reduce_scatter | solution.py:48
  373.5 1.2 convert_element_type.13
  374.7 0.9 copy.36
  (1 shorter events, 0.0 us)
Async XLA Ops:
  7.2 1.1 copy-start
  7.2 190.3 %reduce-scatter.3.cloned.1.call-start = ((), (), s32[]{:S(2)}) async-start(), calls=%async_computation.4 | async-start | bytes 8912896 | tf_op jit(solution)/shard_map/reduce_scatter | solution.py:19
  16.8 340.2 %all-gather.2.cloned.1.call-start = ((), (), s32[]{:S(2)}) async-start(), calls=%async_computation.5 | async-start | bytes 4456448 | tf_op jit(solution)/shard_map/all_gather | solution.py:44
  234.2 5.8 %copy-start.1 = (bf16[8,512,512]{2,1,0:T(8,128)(2,1)S(1)}, bf16[8,512,512]{2,1,0:T(8,128)(2,1)}, u32[]{:S(2)}) copy-start(bf16[8,512,512]{2,1,0:T(8,128)(2,1)} %param.11) | copy-start | bytes 12582916
  239.3 0.8 copy-start.2
  273.5 8.3 %copy-start.4 = (bf16[32,4096]{1,0:T(8,128)(2,1)S(1)}, bf16[32,4096]{1,0:T(8,128)(2,1)}, u32[]{:S(2)}) copy-start(bf16[32,4096]{1,0:T(8,128)(2,1)} %param.9) | copy-start | bytes 786436
  282.5 83.2 %copy-start.3 = (f32[32,8,512]{2,0,1:T(8,128)S(1)}, f32[32,8,512]{2,0,1:T(8,128)}, u32[]{:S(2)}) copy-start(f32[32,8,512]{2,0,1:T(8,128)} %copy-done.2) | copy-start | bytes 1572868
  282.5 91.0 %reduce-scatter.5.cloned.1.call-start = ((), (), s32[]{:S(2)}) async-start(), calls=%async_computation.6 | async-start | bytes 2359296 | tf_op jit(solution)/shard_map/reduce_scatter | solution.py:48
Sparse Core Ops, SparseCore 0:
  16.9 180.5 reduce-scatter.2
  282.6 74.3 all-gather.1
  365.8 7.6 reduce-scatter.4
where the time goes:
time: 383 us; the launch traced here: 382 us
  waiting for transfers between devices  261 us (68%)
  blocking collectives  41 us (11%)
  matrix products  36.9 us (10%)
  local copies, waits for them, and re-layouts  22.9 us (6%)
  between operations  13.9 us (4%)
  other arithmetic  6.59 us (2%)
    reduce_scatter x1, waiting for transfers between devices, local(): lax.psum_scatter(lax.dot_general(out_grads, activations, (((0,), (0,)), (...  181 us
    all_gather x1, waiting for transfers between devices, local(): lax.all_gather(new_weight, 'dp', axis=0, tiled=True)  74.4 us
    all_to_all x1, blocking collectives, local(): lax.all_to_all(left_turned, 'dp', split_axis=2, concat_axis=0, tiled=True)  22.7 us
    all_to_all x1, blocking collectives, local(): lax.all_to_all(back_turned, 'dp', split_axis=2, concat_axis=0, tiled=True)  18.3 us
    unnamed x17, local copies, waits for them, and re-layouts  10 us
    dot_general x1, matrix products, local(): lax.dot_general(activations, lax.all_gather(new_weight, 'dp', axis=0, til...  8.69 us
    dot_general x1, matrix products, local(): lax.dot_general(out_grads, activations, (((0,), (0,)), ((), ())), preferr...  8.44 us
  transfers between devices with their start and end apart: 3, of which 3 were waited for; matrix products, arithmetic and copies ran while one was open for 1% of the time, Pallas kernels for 0%

commit v1 on v0

--- a/solution.py
+++ b/solution.py
@@ -1,6 +1,8 @@
 import jax
 import jax.numpy as jnp
 from jax import lax
+from jax.experimental import pallas as pl
+from jax.experimental.pallas import tpu as pltpu
 from jax.sharding import PartitionSpec as P
 
 STEP = 10
@@ -8,6 +10,9 @@
 
 LEARNING_RATE = 0.02
 epsilon = 1e-08
+MESH = pl.DeviceIdType.MESH
+BF = jnp.bfloat16
+F32 = jnp.float32
 
 
 def local(activations, out_grads, weight, left_basis, right_basis, first_moment, second_moment):
@@ -51,6 +56,333 @@
     return (layer_output, new_weight, new_first, new_second)
 
 
+def split_dot(values, basis, dims):
+    high = values.astype(BF)
+    low = (values - high.astype(F32)).astype(BF)
+    return lax.dot_general(high, basis, dims, preferred_element_type=F32) + lax.dot_general(
+        low, basis, dims, preferred_element_type=F32
+    )
+
+
+ROWS_COLS = (((1,), (0,)), ((), ()))
+ROWS_ROWS = (((1,), (1,)), ((), ()))
+
+
+def kernel(
+    act_h, og_h, w_h, left_h, right_h, m_h, v_h,
+    out_h, nw_h, nf_h, ns_h,
+    act, og, w, left, right, m, v, turned,
+    s1, r1, keep1, s2, r2, keep2, zs, zr, slab,
+    a_send, a_recv, b_send, b_recv, flip, nf, ns,
+    full, po, po_recv, out,
+    load_sem, act_sem, store_sem,
+    s1_sem, r1_sem, s2_sem, r2_sem, zs_sem, zr_sem,
+    as_sem, ar_sem, bs_sem, br_sem,
+    gz_s, gz_r, gx_s, gx_r, gy_s, gy_r, gf_s, gf_r, c_s, c_r,
+):
+    me = lax.axis_index("dp")
+    core = lax.axis_index("cuts")
+    z, plane = me // 4, me % 4
+    bits = (me % 2, (me // 2) % 2)
+    n = 16
+    nb = 8
+    near = (me + 1 - 2 * bits[0], me + 2 - 4 * bits[1])
+
+    def remote(src, dst, ss, rs, target):
+        return pltpu.make_async_remote_copy(
+            src_ref=src, dst_ref=dst, send_sem=ss, recv_sem=rs,
+            device_id=(target, core), device_id_type=MESH,
+        )
+
+    acts = [
+        pltpu.make_async_copy(
+            act_h.at[:, pl.ds(i * 512, 512)], act.at[:, pl.ds(i * 512, 512)], act_sem.at[i]
+        )
+        for i in range(nb)
+    ]
+    loads = [
+        pltpu.make_async_copy(a, b, load_sem.at[i])
+        for i, (a, b) in enumerate(
+            ((og_h, og), (left_h, left), (right_h, right), (m_h, m), (v_h, v), (w_h, w))
+        )
+    ]
+    loads[0].start()
+    for c in acts + loads[1:]:
+        c.start()
+
+    barrier = pltpu.get_barrier_semaphore()
+    for j in range(1, n):
+        pl.semaphore_signal(
+            barrier, inc=1, device_id=(lax.rem(me + j, n), core), device_id_type=MESH
+        )
+    pl.semaphore_signal(barrier, inc=1, device_id=(me, 1 - core), device_id_type=MESH)
+
+    loads[0].wait()
+    across = og[...].T
+    for zz in range(4):
+        for yy in range(2):
+            for xx in range(2):
+                at = zz * 128 + yy * 64 + xx * 32
+                piece = across[at : at + 32]
+                turned[0, xx, pl.ds(yy * 128 + zz * 32, 32)] = piece
+                turned[1, yy, pl.ds(xx * 128 + zz * 32, 32)] = piece
+    pl.semaphore_wait(barrier, n)
+
+    pending = []
+
+    first = []
+    for i in range(nb):
+        h = i % 2
+        acts[i].wait()
+        block = act[:, i * 512 : (i + 1) * 512]
+        s1[i] = (
+            lax.dot_general(turned[h, 1 - bits[h]], block, ROWS_COLS, preferred_element_type=F32)
+            .astype(BF)
+            .reshape(2, 128, 512)
+        )
+        copy = remote(s1.at[i], r1.at[i], s1_sem.at[i], r1_sem.at[i], near[h])
+        copy.start()
+        first.append(copy)
+        keep1[i] = lax.dot_general(
+            turned[h, bits[h]], block, ROWS_COLS, preferred_element_type=F32
+        ).reshape(2, 128, 512)
+    pending += first
+
+    second = []
+
+    def stage2(i):
+        h = i % 2
+        b = bits[1 - h]
+        first[i].wait_recv()
+        s2[i] = (keep1[i, 1 - b] + r1[i, 1 - b].astype(F32)).astype(BF).reshape(4, 32, 512)
+        copy = remote(s2.at[i], r2.at[i], s2_sem.at[i], r2_sem.at[i], near[1 - h])
+        copy.start()
+        second.append(copy)
+        pending.append(copy)
+        keep2[i] = (keep1[i, b] + r1[i, b].astype(F32)).reshape(4, 32, 512)
+
+    third = {}
+
+    def stage3(i):
+        second[i].wait_recv()
+        for j in (2, 1, 3):
+            to = lax.rem(z + j, 4)
+            zs[i, j - 1] = (keep2[i, to] + r2[i, to].astype(F32)).astype(BF)
+            copy = remote(
+                zs.at[i, j - 1], zr.at[i, j - 1], zs_sem.at[i, j - 1], zr_sem.at[i, j - 1],
+                to * 4 + plane,
+            )
+            copy.start()
+            third[i, j] = copy
+            pending.append(copy)
+
+    def finish(i):
+        total = keep2[i, z] + r2[i, z].astype(F32)
+        for j in (1, 2, 3):
+            third[i, j].wait_recv()
+            total = total + zr[i, j - 1].astype(F32)
+        if i == 0:
+            loads[1].wait()
+        slab[i] = split_dot(total, left[i], ROWS_COLS)
+
+    def pack(buffer, group):
+        blocks = [slab[4 * group + q] for q in range(4)]
+        for d in range(n):
+            buffer[group, d] = jnp.concatenate(
+                [b[:, d * 32 : d * 32 + 32] for b in blocks], axis=1
+            ).astype(BF)
+
+    def send_all(buffer, landing, ss, rs, group):
+        copies = []
+        for j in range(1, n):
+            to = lax.rem(me + j, n)
+            copy = remote(
+                buffer.at[group, to], landing.at[group, me], ss.at[group, j - 1],
+                rs.at[group, j - 1], to,
+            )
+            copy.start()
+            copies.append(copy)
+        landing[group, me] = buffer[group, me]
+        pending.extend(copies)
+        return copies
+
+    a_copies = {}
+    for t in range(nb + 4):
+        if t < nb:
+            stage2(t)
+        if 0 <= t - 2 < nb:
+            stage3(t - 2)
+        if 0 <= t - 4 < nb:
+            finish(t - 4)
+            if (t - 4) % 4 == 3:
+                group = (t - 4) // 4
+                pack(a_send, group)
+                a_copies[group] = send_all(a_send, a_recv, as_sem, ar_sem, group)
+
+    for c in loads[2:]:
+        c.wait()
+
+    bias_first = 1.0 - 0.9**STEP
+    bias_second = 1.0 - 0.95**STEP
+    b_copies = {}
+    for group in range(2):
+        for c in a_copies[group]:
+            c.wait_recv()
+        flip[...] = a_recv[group].reshape(512, 128).T
+        for q in range(4):
+            g = 4 * group + q
+            rotated = lax.dot_general(
+                flip[q * 32 : q * 32 + 32], right[g], ROWS_COLS, preferred_element_type=F32
+            )
+            new_first = 0.9 * m[:, g, :] + 0.1 * rotated
+            new_second = 0.95 * v[:, g, :] + 0.05 * rotated * rotated
+            nf[:, g, :] = new_first
+            ns[:, g, :] = new_second
+            direction = new_first / bias_first / (jnp.sqrt(new_second / bias_second) + epsilon)
+            slab[g] = split_dot(direction, right[g], ROWS_ROWS)
+        pack(b_send, group)
+        b_copies[group] = send_all(b_send, b_recv, bs_sem, br_sem, group)
+
+    stores = [
+        pltpu.make_async_copy(nf, nf_h, store_sem.at[0]),
+        pltpu.make_async_copy(ns, ns_h, store_sem.at[1]),
+    ]
+    for c in stores:
+        c.start()
+
+    def part(index, h):
+        return full.at[index, :, pl.ds(h * 2048, 2048)]
+
+    from_z, from_x, from_y, passed = {}, {}, {}, {}
+
+    def spread(h, jj):
+        index = lax.rem(z + 4 - jj, 4) * 4 + plane
+        piece = part(index, h)
+        from_x[h, jj] = remote(piece, piece, gx_s.at[h, jj], gx_r.at[h, jj], near[0])
+        from_y[h, jj] = remote(piece, piece, gy_s.at[h, jj], gy_r.at[h, jj], near[1])
+        from_x[h, jj].start()
+        from_y[h, jj].start()
+        pending.extend([from_x[h, jj], from_y[h, jj]])
+
+    def forward(h, jj):
+        row = lax.rem(z + 4 - jj, 4) * 4
+        if h == 0:
+            from_y[h, jj].wait_recv()
+            piece = part(row + (near[1] % 4), h)
+            target = near[0]
+        else:
+            from_x[h, jj].wait_recv()
+            piece = part(row + (near[0] % 4), h)
+            target = near[1]
+        passed[h, jj] = remote(piece, piece, gf_s.at[h, jj], gf_r.at[h, jj], target)
+        passed[h, jj].start()
+        pending.append(passed[h, jj])
+
+    for h in range(2):
+        for c in b_copies[h]:
+            c.wait_recv()
+        flip[...] = b_recv[h].reshape(512, 128).T
+        for q in range(4):
+            g = 4 * h + q
+            update = lax.dot_general(
+                flip[q * 32 : q * 32 + 32], left[g], ROWS_ROWS, preferred_element_type=F32
+            )
+            columns = slice(g * 512, (g + 1) * 512)
+            full[me, :, columns] = (
+                w[:, columns].astype(F32) - LEARNING_RATE * update
+            ).astype(BF)
+        for jj in (2, 1, 3):
+            piece = part(me, h)
+            from_z[h, jj] = remote(
+                piece, piece, gz_s.at[h, jj - 1], gz_r.at[h, jj - 1], lax.rem(z + jj, 4) * 4 + plane
+            )
+            from_z[h, jj].start()
+            pending.append(from_z[h, jj])
+        spread(h, 0)
+
+    stores.append(pltpu.make_async_copy(full.at[me], nw_h, store_sem.at[2]))
+    stores[2].start()
+
+    def product(jj):
+        row = lax.rem(z + 4 - jj, 4)
+        for h in range(2):
+            (from_x if h == 0 else from_y)[h, jj].wait_recv()
+            passed[h, jj].wait_recv()
+        po[row] = lax.dot_general(
+            act[...], full[pl.ds(row * 4, 4)].reshape(128, 4096), ROWS_ROWS,
+            preferred_element_type=F32,
+        )
+
+    order = (0, 1, 3, 2)
+    for a, jj in enumerate(order):
+        for h in range(2):
+            if jj:
+                from_z[h, jj].wait_recv()
+                spread(h, jj)
+            if a:
+                forward(h, order[a - 1])
+        if a > 1:
+            product(order[a - 2])
+    for h in range(2):
+        forward(h, order[3])
+    product(order[2])
+    product(order[3])
+
+    swap = pltpu.make_async_remote_copy(
+        src_ref=po.at[pl.ds(2 - 2 * core, 2)], dst_ref=po_recv, send_sem=c_s, recv_sem=c_r,
+        device_id=(me, 1 - core), device_id_type=MESH,
+    )
+    swap.start()
+    for c in pending:
+        c.wait_send()
+    swap.wait_recv()
+    for k in range(2):
+        out[:, k * 128 : (k + 1) * 128] = (po[2 * core + k] + po_recv[k]).astype(BF)
+    stores.append(pltpu.make_async_copy(out, out_h, store_sem.at[3]))
+    stores[3].start()
+    swap.wait_send()
+    for c in stores:
+        c.wait()
+
+
+def fused(activations, out_grads, weight, left_basis, right_basis, first_moment, second_moment):
+    any_space = pl.BlockSpec(memory_space=pl.ANY)
+    dma = pltpu.SemaphoreType.DMA
+    vm = pltpu.VMEM
+    return pl.pallas_call(
+        kernel,
+        out_shape=(
+            jax.ShapeDtypeStruct((768, 256), BF),
+            jax.ShapeDtypeStruct((32, 4096), BF),
+            jax.ShapeDtypeStruct((32, 8, 512), F32),
+            jax.ShapeDtypeStruct((32, 8, 512), F32),
+        ),
+        in_specs=[any_space] * 7,
+        out_specs=(any_space,) * 4,
+        scratch_shapes=[
+            vm((768, 4096), BF), vm((768, 512), BF), vm((32, 4096), BF),
+            vm((8, 512, 512), BF), vm((8, 512, 512), BF),
+            vm((32, 8, 512), F32), vm((32, 8, 512), F32), vm((2, 2, 256, 768), BF),
+            vm((8, 2, 128, 512), BF), vm((8, 2, 128, 512), BF), vm((8, 2, 128, 512), F32),
+            vm((8, 4, 32, 512), BF), vm((8, 4, 32, 512), BF), vm((8, 4, 32, 512), F32),
+            vm((8, 3, 32, 512), BF), vm((8, 3, 32, 512), BF), vm((8, 32, 512), F32),
+            vm((2, 16, 32, 128), BF), vm((2, 16, 32, 128), BF),
+            vm((2, 16, 32, 128), BF), vm((2, 16, 32, 128), BF),
+            vm((128, 512), BF), vm((32, 8, 512), F32), vm((32, 8, 512), F32),
+            vm((16, 32, 4096), BF), vm((4, 768, 128), F32), vm((2, 768, 128), F32),
+            vm((768, 256), BF),
+            dma((6,)), dma((8,)), dma((4,)),
+            dma((8,)), dma((8,)), dma((8,)), dma((8,)), dma((8, 3)), dma((8, 3)),
+            dma((2, 15)), dma((2, 15)), dma((2, 15)), dma((2, 15)),
+            dma((2, 3)), dma((2, 3)), dma((2, 4)), dma((2, 4)), dma((2, 4)), dma((2, 4)),
+            dma((2, 4)), dma((2, 4)), dma, dma,
+        ],
+        compiler_params=pltpu.CompilerParams(
+            collective_id=0, has_side_effects=True, vmem_limit_bytes=60 * 1024 * 1024
+        ),
+    )(activations, out_grads, weight, left_basis, right_basis, first_moment, second_moment)
+
+
 def solution(mesh):
     placed = (
         P("dp", "cuts"),
@@ -61,8 +393,9 @@
         P("dp", "cuts", None),
         P("dp", "cuts", None),
     )
+    small = mesh.shape["dp"] == 16 and mesh.shape["cuts"] == 2
     return jax.shard_map(
-        local,
+        fused if small else local,
         mesh=mesh,
         in_specs=placed,
         out_specs=(P("dp", "cuts"), P("dp", "cuts"), P("dp", "cuts", None), P("dp", "cuts", None)),

time: 383 us -> 136 us (0.36)
  the two profiles are of different devices: /device:TPU:0 before, /device:TPU:23 now
where the time goes in v1:
time: 136 us
  Pallas kernels  128 us (94%)
  local copies, waits for them, and re-layouts  7.17 us (5%)
    pallas_call x1, Pallas kernels, fused(): pl.pallas_call(kernel, out_shape=(jax.ShapeDtypeStruct((768, 256), BF), j...  128 us
    unnamed x4, local copies, waits for them, and re-layouts  7.17 us

profile of v1, /device:TPU:23, one launch (start us, length us, event | category | flops | bytes accessed | tf_op | source)
XLA Modules:
  0.0 136.1 jit_solution(13385374455594679828)
XLA Ops:
  0.6 128.3 %shard_map.102 = (bf16[768,256]{1,0:T(8,128)(2,1)}, bf16[32,4096]{1,0:T(8,128)(2,1)}, f32[32,8,512]{2,1,0:T(8,128)}, f32[32,8,512]{2,1,0:T(8,128)}) custom-call(bf16[768,4096]{1,0:T(8,128)(2,1)} %act_h.1, bf16[768,512]{1,0:T(8,128)(2,1)} %og_h.1, bf16[32,4096]{1,0:T(8,128)(2,1)} %w_h.1, bf16[8,512,512]{2,1,0:T(8,128)(2,1)} %left_h.1, ...), custom_call_target="tpu_custom_call" | custom-call | tf_op jit(solution)/shard_map/pallas_call | solution.py:352
  128.9 1.8 %copy.15 = bf16[768,256]{1,0:T(8,128)(2,1)} copy(bf16[768,256]{1,0:T(8,128)(2,1)} %get-tuple-element.8) | data formatting | bytes 786432
  130.7 1.7 %copy.16 = bf16[32,4096]{1,0:T(8,128)(2,1)} copy(bf16[32,4096]{1,0:T(8,128)(2,1)} %get-tuple-element.9) | data formatting | bytes 524288
  132.4 1.9 %copy.17 = f32[32,8,512]{2,1,0:T(8,128)} copy(f32[32,8,512]{2,1,0:T(8,128)} %get-tuple-element.10) | data formatting | bytes 1048576
  134.2 1.9 %copy.18 = f32[32,8,512]{2,1,0:T(8,128)} copy(f32[32,8,512]{2,1,0:T(8,128)} %get-tuple-element.11) | data formatting | bytes 1048576

commit v2 on v1

--- a/solution.py
+++ b/solution.py
@@ -126,7 +126,6 @@
                 piece = across[at : at + 32]
                 turned[0, xx, pl.ds(yy * 128 + zz * 32, 32)] = piece
                 turned[1, yy, pl.ds(xx * 128 + zz * 32, 32)] = piece
-    pl.semaphore_wait(barrier, n)
 
     pending = []
 
@@ -140,13 +139,18 @@
             .astype(BF)
             .reshape(2, 128, 512)
         )
-        copy = remote(s1.at[i], r1.at[i], s1_sem.at[i], r1_sem.at[i], near[h])
-        copy.start()
-        first.append(copy)
+        first.append(remote(s1.at[i], r1.at[i], s1_sem.at[i], r1_sem.at[i], near[h]))
+        if i == 0:
+            pl.semaphore_wait(barrier, n)
+        if i < 4:
+            first[i].start()
         keep1[i] = lax.dot_general(
             turned[h, bits[h]], block, ROWS_COLS, preferred_element_type=F32
         ).reshape(2, 128, 512)
     pending += first
+
+    def first_start(i):
+        first[i].start()
 
     second = []
 
@@ -207,17 +211,22 @@
         return copies
 
     a_copies = {}
-    for t in range(nb + 4):
-        if t < nb:
-            stage2(t)
-        if 0 <= t - 2 < nb:
-            stage3(t - 2)
-        if 0 <= t - 4 < nb:
-            finish(t - 4)
-            if (t - 4) % 4 == 3:
-                group = (t - 4) // 4
-                pack(a_send, group)
-                a_copies[group] = send_all(a_send, a_recv, as_sem, ar_sem, group)
+
+    def regroup(group):
+        pack(a_send, group)
+        a_copies[group] = send_all(a_send, a_recv, as_sem, ar_sem, group)
+
+    for act_on, pair in (
+        (stage2, 0), (first_start, 4), (stage2, 2), (first_start, 6), (stage3, 0), (stage2, 4),
+        (stage3, 2), (finish, 0), (stage2, 6), (stage3, 4), (finish, 2),
+    ):
+        act_on(pair)
+        act_on(pair + 1)
+    regroup(0)
+    for act_on, pair in ((stage3, 6), (finish, 4), (finish, 6)):
+        act_on(pair)
+        act_on(pair + 1)
+    regroup(1)
 
     for c in loads[2:]:
         c.wait()
@@ -253,10 +262,11 @@
     def part(index, h):
         return full.at[index, :, pl.ds(h * 2048, 2048)]
 
+    meets = (z, z + 1 - 2 * (z % 2), lax.rem(z + 2, 4), 3 - z)
     from_z, from_x, from_y, passed = {}, {}, {}, {}
 
     def spread(h, jj):
-        index = lax.rem(z + 4 - jj, 4) * 4 + plane
+        index = meets[jj] * 4 + plane
         piece = part(index, h)
         from_x[h, jj] = remote(piece, piece, gx_s.at[h, jj], gx_r.at[h, jj], near[0])
         from_y[h, jj] = remote(piece, piece, gy_s.at[h, jj], gy_r.at[h, jj], near[1])
@@ -265,7 +275,7 @@
         pending.extend([from_x[h, jj], from_y[h, jj]])
 
     def forward(h, jj):
-        row = lax.rem(z + 4 - jj, 4) * 4
+        row = meets[jj] * 4
         if h == 0:
             from_y[h, jj].wait_recv()
             piece = part(row + (near[1] % 4), h)
@@ -291,42 +301,44 @@
             full[me, :, columns] = (
                 w[:, columns].astype(F32) - LEARNING_RATE * update
             ).astype(BF)
-        for jj in (2, 1, 3):
+        spread(h, 0)
+        for jj in (1, 2, 3):
             piece = part(me, h)
             from_z[h, jj] = remote(
-                piece, piece, gz_s.at[h, jj - 1], gz_r.at[h, jj - 1], lax.rem(z + jj, 4) * 4 + plane
+                piece, piece, gz_s.at[h, jj - 1], gz_r.at[h, jj - 1], meets[jj] * 4 + plane
             )
             from_z[h, jj].start()
             pending.append(from_z[h, jj])
-        spread(h, 0)
 
     stores.append(pltpu.make_async_copy(full.at[me], nw_h, store_sem.at[2]))
     stores[2].start()
 
     def product(jj):
-        row = lax.rem(z + 4 - jj, 4)
+        row = meets[jj]
+        halves = []
         for h in range(2):
             (from_x if h == 0 else from_y)[h, jj].wait_recv()
             passed[h, jj].wait_recv()
-        po[row] = lax.dot_general(
-            act[...], full[pl.ds(row * 4, 4)].reshape(128, 4096), ROWS_ROWS,
-            preferred_element_type=F32,
-        )
-
-    order = (0, 1, 3, 2)
-    for a, jj in enumerate(order):
+            halves.append(
+                lax.dot_general(
+                    act[:, h * 2048 : (h + 1) * 2048],
+                    full[pl.ds(row * 4, 4), :, h * 2048 : (h + 1) * 2048].reshape(128, 2048),
+                    ROWS_ROWS,
+                    preferred_element_type=F32,
+                )
+            )
+        po[row] = halves[0] + halves[1]
+
+    for jj in range(4):
         for h in range(2):
             if jj:
                 from_z[h, jj].wait_recv()
                 spread(h, jj)
-            if a:
-                forward(h, order[a - 1])
-        if a > 1:
-            product(order[a - 2])
-    for h in range(2):
-        forward(h, order[3])
-    product(order[2])
-    product(order[3])
+        for h in range(2):
+            forward(h, jj)
+        if jj:
+            product(jj - 1)
+    product(3)
 
     swap = pltpu.make_async_remote_copy(
         src_ref=po.at[pl.ds(2 - 2 * core, 2)], dst_ref=po_recv, send_sem=c_s, recv_sem=c_r,
@@ -345,11 +357,16 @@
         c.wait()
 
 
+def hand_over(*refs):
+    for source, target in zip(refs[:4], refs[4:]):
+        target[...] = source[...]
+
+
 def fused(activations, out_grads, weight, left_basis, right_basis, first_moment, second_moment):
     any_space = pl.BlockSpec(memory_space=pl.ANY)
     dma = pltpu.SemaphoreType.DMA
     vm = pltpu.VMEM
-    return pl.pallas_call(
+    results = pl.pallas_call(
         kernel,
         out_shape=(
             jax.ShapeDtypeStruct((768, 256), BF),
@@ -383,6 +400,12 @@
     )(activations, out_grads, weight, left_basis, right_basis, first_moment, second_moment)
 
 
+    return pl.pallas_call(
+        hand_over,
+        out_shape=tuple(jax.ShapeDtypeStruct(r.shape, r.dtype) for r in results),
+    )(*results)
+
+
 def solution(mesh):
     placed = (
         P("dp", "cuts"),

time: 136 us -> 118 us (0.87)
  the two profiles are of different devices: /device:TPU:23 before, /device:TPU:0 now
where the time goes in v2:
time: 118 us; the launch traced here: 116 us
  Pallas kernels  116 us (98%)
    pallas_call x1, Pallas kernels, fused(): pl.pallas_call(kernel, out_shape=(jax.ShapeDtypeStruct((768, 256), BF), j...  113 us
    pallas_call x1, Pallas kernels, fused(): pl.pallas_call(hand_over, out_shape=tuple((jax.ShapeDtypeStruct(r.shape,...  2.6 us

profile of v2, /device:TPU:0, one launch (start us, length us, event | category | flops | bytes accessed | tf_op | source)
XLA Modules:
  0.0 116.3 jit_solution(3736418131640306034)
XLA Ops:
  0.6 113.1 %shard_map.102 = (bf16[768,256]{1,0:T(8,128)(2,1)}, bf16[32,4096]{1,0:T(8,128)(2,1)}, f32[32,8,512]{2,1,0:T(8,128)}, f32[32,8,512]{2,1,0:T(8,128)}) custom-call(bf16[768,4096]{1,0:T(8,128)(2,1)} %act_h.1, bf16[768,512]{1,0:T(8,128)(2,1)} %og_h.1, bf16[32,4096]{1,0:T(8,128)(2,1)} %w_h.1, bf16[8,512,512]{2,1,0:T(8,128)(2,1)} %left_h.1, ...), custom_call_target="tpu_custom_call" | custom-call | tf_op jit(solution)/shard_map/pallas_call | solution.py:369
  113.7 2.6 %shard_map.103 = (bf16[768,256]{1,0:T(8,128)(2,1)}, bf16[32,4096]{1,0:T(8,128)(2,1)}, f32[32,8,512]{2,1,0:T(8,128)}, f32[32,8,512]{2,1,0:T(8,128)}) custom-call(bf16[768,256]{1,0:T(8,128)(2,1)} %get-tuple-element.8.refs_0_, bf16[32,4096]{1,0:T(8,128)(2,1)} %get-tuple-element.9.refs_1_, f32[32,8,512]{2,1,0:T(8,128)} %get-tuple-element.10.refs_2_, ...), custom_call_target="tpu_custom_call" | custom-call | tf_op jit(solution)/shard_map/pallas_call | solution.py:403
